TPU v7x, 32 devices: a whole 2x2x4 slice. The times are simulated.
32 devices in a mesh: src: 4 (over y, x), tgt: 8 (over z, core).
Axes of the slice: x: 2, y: 2, z: 4, core: 2. Of those that a mesh axis runs over, the one named last changes fastest.
Arguments:
- sources: bfloat16 [32768, 64], P(('src', 'tgt'))
- targets: bfloat16 [65536, 64], P(('src', 'tgt'))
- log_src: float32 [32768], P(('src', 'tgt')), may hold values from -1 to 1
- log_tgt: float32 [65536], P(('src', 'tgt')), may hold values from -1 to 1
- tile_rows: int32 [4, 8, 256], P('src', 'tgt'), may hold values from 0 to 63, as said below
- tile_cols: int32 [4, 8, 256], P('src', 'tgt'), may hold values from 0 to 63, as said below
- tile_count: int32 [4, 8], P('src', 'tgt'), may hold values from 64 to 256, as said below
Outputs:
- src_potential: float32 [32768], P(('src', 'tgt'))
- tgt_potential: float32 [65536], P(('src', 'tgt'))
Inputs may be any that keep to these rules, and one draw needn't show every extreme that they name: `tile_rows`: each entry is a block number within the group. `tile_cols`: each entry is a block number within the group; within one pair of groups no (row, column) pair of blocks appears twice among all 256 slots; among the live slots of every pair of groups every source block and every target block appears. `tile_count`: some pair of groups has exactly 256 live slots and some other exactly 64.
All inputs are finite; a program needn't handle non-finite values.
Results may differ from a plain program's by a relative error of at most 0.00075.
Values may be sent and summed in bfloat16 or wider, within the bound.
A program may use at most 64 MiB of HBM per device.

v0:
```python
import jax
import jax.numpy as jnp
from jax import lax
from jax.sharding import PartitionSpec as P

TILE = 128
ITERS = 3


EPS_BLUR = 0.1
NEG_FLOOR = -1e30
tile_group = 16


def point_norms(points):
    widened = points.astype(jnp.float32)
    return jnp.sum(widened * widened, axis=-1)


def tile_scores(near_points, near_norms, far_points, far_norms, far_potential):
    cross = jnp.einsum("kif,kjf->kij", near_points, far_points, preferred_element_type=jnp.float32)
    costs = (near_norms[:, :, None] + far_norms[:, None, :] - 2.0 * cross) * (
        1.0 / near_points.shape[-1]
    )
    return (far_potential[:, None, :] - costs) / EPS_BLUR


def fold_stats(highest, summed, scores, near_index, active):
    active_tile = active[:, None, None]
    masked = jnp.where(active_tile, scores, NEG_FLOOR)
    tile_high = jnp.max(masked, axis=2)
    new_high = highest.at[near_index].max(tile_high)
    weights = jnp.exp(masked - new_high[near_index][:, :, None]) * active_tile.astype(jnp.float32)
    added = jnp.zeros_like(summed).at[near_index].add(jnp.sum(weights, axis=2))
    return (new_high, summed * jnp.exp(highest - new_high) + added)


def local_stats(
    near_blocks, near_norms, far_blocks, far_norms, far_potential, near_lists, far_lists, active
):

    def visit(group_index, state_pair):
        offset = group_index * tile_group
        near_index = lax.dynamic_slice_in_dim(near_lists, offset, tile_group)
        far_index = lax.dynamic_slice_in_dim(far_lists, offset, tile_group)
        active_part = lax.dynamic_slice_in_dim(active, offset, tile_group)
        scores = tile_scores(
            near_blocks[near_index],
            near_norms[near_index],
            far_blocks[far_index],
            far_norms[far_index],
            far_potential[far_index],
        )
        return fold_stats(state_pair[0], state_pair[1], scores, near_index, active_part)

    initial = (
        jnp.full(near_norms.shape, NEG_FLOOR, jnp.float32),
        jnp.zeros(near_norms.shape, jnp.float32),
    )
    return lax.fori_loop(0, near_lists.shape[0] // tile_group, visit, initial)


def settle(highest, summed, logs, along_rows):
    if along_rows:
        peak_all = lax.pmax(highest, "tgt")
        sum_all = lax.psum(summed * jnp.exp(highest - peak_all), "tgt")
    else:
        peak_all = lax.pmax(highest, "src")
        sum_all = lax.psum(summed * jnp.exp(highest - peak_all), "src")
    return EPS_BLUR * (logs - (peak_all + jnp.log(sum_all)))


def local(sources, targets, log_src, log_tgt, tile_rows, tile_cols, tile_count):
    src_points, src_logs = (
        lax.all_gather(sources, "tgt", axis=0, tiled=True),
        lax.all_gather(log_src.astype(jnp.bfloat16), "tgt", axis=0, tiled=True).astype(
            log_src.dtype
        ),
    )
    tgt_points, tgt_logs = (
        lax.all_gather(targets, "src", axis=0, tiled=True),
        lax.all_gather(log_tgt.astype(jnp.bfloat16), "src", axis=0, tiled=True).astype(
            log_tgt.dtype
        ),
    )
    src_blocks = src_points.reshape(-1, TILE, src_points.shape[1])
    tgt_blocks = tgt_points.reshape(-1, TILE, tgt_points.shape[1])
    src_norms = point_norms(src_blocks)
    tgt_norms = point_norms(tgt_blocks)
    row_lists = tile_rows.reshape(-1)
    col_lists = tile_cols.reshape(-1)
    active = lax.iota(jnp.int32, row_lists.shape[0]) < tile_count.reshape(())
    tgt_potential = jnp.zeros(tgt_norms.shape, jnp.float32)
    src_potential = jnp.zeros(src_norms.shape, jnp.float32)
    for sweep_index in range(ITERS):
        highest, summed = local_stats(
            src_blocks,
            src_norms,
            tgt_blocks,
            tgt_norms,
            tgt_potential,
            row_lists,
            col_lists,
            active,
        )
        src_potential = settle(highest.reshape(-1), summed.reshape(-1), src_logs, True).reshape(
            src_norms.shape
        )
        highest, summed = local_stats(
            tgt_blocks,
            tgt_norms,
            src_blocks,
            src_norms,
            src_potential,
            col_lists,
            row_lists,
            active,
        )
        tgt_potential = settle(highest.reshape(-1), summed.reshape(-1), tgt_logs, False).reshape(
            tgt_norms.shape
        )
    src_share = sources.shape[0]
    tgt_share = targets.shape[0]
    src_out = lax.dynamic_slice_in_dim(
        src_potential.reshape(-1), lax.axis_index("tgt") * src_share, src_share
    )
    tgt_out = lax.dynamic_slice_in_dim(
        tgt_potential.reshape(-1), lax.axis_index("src") * tgt_share, tgt_share
    )
    return (src_out, tgt_out)


def solution(mesh):
    in_specs = (
        P(("src", "tgt"), None),
        P(("src", "tgt"), None),
        P(("src", "tgt")),
        P(("src", "tgt")),
        P("src", "tgt", None),
        P("src", "tgt", None),
        P("src", "tgt"),
    )
    out_specs = (P(("src", "tgt")), P(("src", "tgt")))
    return jax.shard_map(local, mesh=mesh, in_specs=in_specs, out_specs=out_specs, check_vma=False)
```

profile of v0, /device:TPU:0, one launch (start us, length us, event | category | flops | bytes accessed | tf_op | source)
XLA Modules:
  0.0 1327.7 jit_solution(3321263258986552720)
XLA Ops:
  10.7 9.6 all_gather.13
  20.3 12.9 all_gather.12
  33.2 6.0 all-gather.5.cloned.1.call-done
  41.6 21.3 %all-gather.3.cloned.1.call-done = bf16[8192,64]{0,1:T(8,128)(2,1)} async-done(((bf16[1024,64]{0,1:T(8,128)(2,1)}), bf16[8192,64]{0,1:T(8,128)(2,1)}) %all-gather.3.cloned.1.call-update) | async-done | bytes 1048592 | tf_op jit(solution)/shard_map/all_gather | solution.py:75
  66.1 167.6 %while.90 = (s32[]{:T(128)}, f32[64,128]{1,0:T(8,128)S(1)}, f32[64,128]{1,0:T(8,128)S(1)}, s32[256]{0:T(256)S(1)}, pred[256]{0:T(512)(128)(4,1)S(1)}, /*index=5*...) while((s32[]{:T(128)}, f32[64,128]{1,0:T(8,128)S(1)}, ...), condition=%wide.region_7.8_spmd, body=%wide.region_2.7_spmd.sunk | while | flops 36456564 | bytes 4138231 | solution.py:60
  233.7 27.6 %pmax.42 = f32[8192]{0:T(1024)S(1)} all-reduce(f32[8192]{0:T(1024)S(1)} %bitcast.82), channel_id=1, replica_groups=mesh['src'=4,'tgt'=8] {'tgt'}, use_global_device_ids=true, to_apply=%region_8.9 | all-reduce | flops 8192 | bytes 65536 | tf_op jit(solution)/shard_map/pmax | solution.py:65
  261.3 25.9 %psum.42 = f32[8192]{0:T(1024)S(1)} all-reduce(f32[8192]{0:T(1024)S(1)} %bitcast_multiply_fusion.5), channel_id=1, replica_groups=mesh['src'=4,'tgt'=8] {'tgt'}, use_global_device_ids=true, to_apply=%region_9.10 | all-reduce | flops 8192 | bytes 65536 | tf_op jit(solution)/shard_map/psum | solution.py:66
  287.3 167.4 %while.91 = (s32[]{:T(128)}, f32[64,128]{1,0:T(8,128)S(1)}, f32[64,128]{1,0:T(8,128)S(1)}, s32[256]{0:T(256)S(1)}, pred[256]{0:T(512)(128)(4,1)S(1)}, /*index=5*...) while((s32[]{:T(128)}, f32[64,128]{1,0:T(8,128)S(1)}, ...), condition=%wide.region_15.16_spmd, body=%wide.region_10.15_spmd.sunk | while | flops 36456564 | bytes 4105459 | solution.py:60
  289.4 3.0 gather_fusion.7
  299.9 3.0 gather_fusion.7
  310.3 3.0 gather_fusion.7
  320.8 3.0 gather_fusion.7
  331.2 3.0 gather_fusion.7
  341.7 3.0 gather_fusion.7
  352.2 3.0 gather_fusion.7
  362.6 3.0 gather_fusion.7
  373.1 3.0 gather_fusion.7
  383.6 3.0 gather_fusion.7
  394.0 3.0 gather_fusion.7
  404.5 3.0 gather_fusion.7
  414.9 3.0 gather_fusion.7
  425.4 3.0 gather_fusion.7
  435.9 3.0 gather_fusion.7
  446.3 3.0 gather_fusion.7
  454.7 16.4 %pmax.43 = f32[8192]{0:T(1024)S(1)} all-reduce(f32[8192]{0:T(1024)S(1)} %bitcast.83), channel_id=1, replica_groups=mesh['src'=4,'tgt'=8] {'src'}, use_global_device_ids=true, to_apply=%region_16.17 | all-reduce | flops 8192 | bytes 65536 | tf_op jit(solution)/shard_map/pmax | solution.py:68
  471.1 14.0 %psum.43 = f32[8192]{0:T(1024)S(1)} all-reduce(f32[8192]{0:T(1024)S(1)} %bitcast_multiply_fusion.4), channel_id=1, replica_groups=mesh['src'=4,'tgt'=8] {'src'}, use_global_device_ids=true, to_apply=%region_17.18 | all-reduce | flops 8192 | bytes 65536 | tf_op jit(solution)/shard_map/psum | solution.py:69
  485.2 167.4 %while.92 = (s32[]{:T(128)}, f32[64,128]{1,0:T(8,128)S(1)}, f32[64,128]{1,0:T(8,128)S(1)}, s32[256]{0:T(256)S(1)}, pred[256]{0:T(512)(128)(4,1)S(1)}, /*index=5*...) while((s32[]{:T(128)}, f32[64,128]{1,0:T(8,128)S(1)}, ...), condition=%wide.region_23.24_spmd, body=%wide.region_18.23_spmd.sunk | while | flops 36456564 | bytes 4105459 | solution.py:60
  652.6 25.9 %pmax.44 = f32[8192]{0:T(1024)S(1)} all-reduce(f32[8192]{0:T(1024)S(1)} %bitcast.84), channel_id=1, replica_groups=mesh['src'=4,'tgt'=8] {'tgt'}, use_global_device_ids=true, to_apply=%region_24.25 | all-reduce | flops 8192 | bytes 65536 | tf_op jit(solution)/shard_map/pmax | solution.py:65
  678.5 25.9 %psum.44 = f32[8192]{0:T(1024)S(1)} all-reduce(f32[8192]{0:T(1024)S(1)} %bitcast_multiply_fusion.3), channel_id=1, replica_groups=mesh['src'=4,'tgt'=8] {'tgt'}, use_global_device_ids=true, to_apply=%region_25.26 | all-reduce | flops 8192 | bytes 65536 | tf_op jit(solution)/shard_map/psum | solution.py:66
  704.5 167.4 %while.93 = (s32[]{:T(128)}, f32[64,128]{1,0:T(8,128)S(1)}, f32[64,128]{1,0:T(8,128)S(1)}, s32[256]{0:T(256)S(1)}, pred[256]{0:T(512)(128)(4,1)S(1)}, /*index=5*...) while((s32[]{:T(128)}, f32[64,128]{1,0:T(8,128)S(1)}, ...), condition=%wide.region_31.32_spmd, body=%wide.region_26.31_spmd.sunk | while | flops 36456564 | bytes 4105459 | solution.py:60
  706.6 3.0 gather_fusion.19
  717.1 3.0 gather_fusion.19
  727.5 3.0 gather_fusion.19
  738.0 3.0 gather_fusion.19
  748.5 3.0 gather_fusion.19
  758.9 3.0 gather_fusion.19
  832.2 3.0 gather_fusion.19
  871.9 16.0 %pmax.45 = f32[8192]{0:T(1024)S(1)} all-reduce(f32[8192]{0:T(1024)S(1)} %bitcast.85), channel_id=1, replica_groups=mesh['src'=4,'tgt'=8] {'src'}, use_global_device_ids=true, to_apply=%region_32.33 | all-reduce | flops 8192 | bytes 65536 | tf_op jit(solution)/shard_map/pmax | solution.py:68
  887.9 14.0 %psum.45 = f32[8192]{0:T(1024)S(1)} all-reduce(f32[8192]{0:T(1024)S(1)} %bitcast_multiply_fusion.2), channel_id=1, replica_groups=mesh['src'=4,'tgt'=8] {'src'}, use_global_device_ids=true, to_apply=%region_33.34 | all-reduce | flops 8192 | bytes 65536 | tf_op jit(solution)/shard_map/psum | solution.py:69
  902.0 167.4 %while.94 = (s32[]{:T(128)}, f32[64,128]{1,0:T(8,128)S(1)}, f32[64,128]{1,0:T(8,128)S(1)}, s32[256]{0:T(256)S(1)}, pred[256]{0:T(512)(128)(4,1)S(1)}, /*index=5*...) while((s32[]{:T(128)}, f32[64,128]{1,0:T(8,128)S(1)}, ...), condition=%wide.region_39.40_spmd, body=%wide.region_34.39_spmd.sunk | while | flops 36456564 | bytes 4105459 | solution.py:60
  1069.4 26.1 %pmax.46 = f32[8192]{0:T(1024)S(1)} all-reduce(f32[8192]{0:T(1024)S(1)} %bitcast.86), channel_id=1, replica_groups=mesh['src'=4,'tgt'=8] {'tgt'}, use_global_device_ids=true, to_apply=%region_40.41 | all-reduce | flops 8192 | bytes 65536 | tf_op jit(solution)/shard_map/pmax | solution.py:65
  1095.5 25.9 %psum.46 = f32[8192]{0:T(1024)S(1)} all-reduce(f32[8192]{0:T(1024)S(1)} %bitcast_multiply_fusion.1), channel_id=1, replica_groups=mesh['src'=4,'tgt'=8] {'tgt'}, use_global_device_ids=true, to_apply=%region_41.42 | all-reduce | flops 8192 | bytes 65536 | tf_op jit(solution)/shard_map/psum | solution.py:66
  1121.5 167.4 %while.95 = (s32[]{:T(128)}, f32[64,128]{1,0:T(8,128)S(1)}, f32[64,128]{1,0:T(8,128)S(1)}, s32[256]{0:T(256)S(1)}, pred[256]{0:T(512)(128)(4,1)S(1)}, /*index=5*...) while((s32[]{:T(128)}, f32[64,128]{1,0:T(8,128)S(1)}, ...), condition=%wide.region_47.48_spmd, body=%wide.region_42.47_spmd.sunk | while | flops 36456564 | bytes 4105459 | solution.py:60
  1123.6 3.0 gather_fusion.31
  1165.4 3.0 gather_fusion.31
  1175.9 3.0 gather_fusion.31
  1288.9 16.8 %pmax.47 = f32[8192]{0:T(1024)S(1)} all-reduce(f32[8192]{0:T(1024)S(1)} %bitcast.81), channel_id=1, replica_groups=mesh['src'=4,'tgt'=8] {'src'}, use_global_device_ids=true, to_apply=%region_48.49 | all-reduce | flops 8192 | bytes 65536 | tf_op jit(solution)/shard_map/pmax | solution.py:68
  1305.7 14.0 %psum.47 = f32[8192]{0:T(1024)S(1)} all-reduce(f32[8192]{0:T(1024)S(1)} %bitcast_multiply_fusion), channel_id=1, replica_groups=mesh['src'=4,'tgt'=8] {'src'}, use_global_device_ids=true, to_apply=%region_49.50 | all-reduce | flops 8192 | bytes 65536 | tf_op jit(solution)/shard_map/psum | solution.py:69
  (1667 shorter events, 927.7 us)
Async XLA Ops:
  7.2 32.0 %all-gather.5.cloned.1.call-start = ((), (), s32[]{:S(2)}) async-start(), calls=%async_computation.1 | async-start | bytes 1310720 | tf_op jit(solution)/shard_map/all_gather | solution.py:81
  7.9 55.0 %all-gather.3.cloned.1.call-start = ((), (), s32[]{:S(2)}) async-start(), calls=%async_computation | async-start | bytes 1179648 | tf_op jit(solution)/shard_map/all_gather | solution.py:75
  39.2 2.1 copy-start
  41.6 24.5 %copy-start.2 = (s32[1,1,256]{2,1,0:T(1,128)S(1)}, s32[1,1,256]{2,1,0:T(1,128)}, u32[]{:S(2)}) copy-start(s32[1,1,256]{2,1,0:T(1,128)} %param.23) | copy-start | bytes 3076
  41.6 24.5 %copy-start.3 = (s32[1,1,256]{2,1,0:T(1,128)S(1)}, s32[1,1,256]{2,1,0:T(1,128)}, u32[]{:S(2)}) copy-start(s32[1,1,256]{2,1,0:T(1,128)} %param.24) | copy-start | bytes 3076
  62.9 2.9 copy-start.1
Sparse Core Ops, SparseCore 0:
  9.8 29.3 all-gather.4
  40.8 22.0 all-gather.2
where the time goes:
time: 1330 us
  local copies, waits for them, and re-layouts  647 us (49%)
  blocking collectives  271 us (20%)
  matrix products  181 us (14%)
  other arithmetic  177 us (13%)
  waiting for transfers between devices  28.7 us (2%)
  between operations  15 us (1%)
    gather x96, local copies, waits for them, and re-layouts, visit(): far_blocks[far_index]  213 us
    gather x96, local copies, waits for them, and re-layouts, visit(): near_blocks[near_index]  212 us
    dot_general x96, matrix products, tile_scores(): jnp.einsum('kif,kjf->kij', near_points, far_points, preferred_element_typ...  181 us
    pmax x3, blocking collectives, settle(): peak_all = lax.pmax(highest, 'tgt')  79.7 us
    psum x3, blocking collectives, settle(): sum_all = lax.psum(summed * jnp.exp(highest - peak_all), 'tgt')  77.8 us
    another operation x96, other arithmetic, fold_stats(): new_high = highest.at[near_index].max(tile_high)  67.9 us
    scatter-add x96, other arithmetic, fold_stats(): added = jnp.zeros_like(summed).at[near_index].add(jnp.sum(weights, axis=2))  67.9 us
    gather x96, local copies, waits for them, and re-layouts, fold_stats(): new_high[near_index][:, :, None]  54 us
  transfers between devices with their start and end apart: 2, of which 2 were waited for; matrix products, arithmetic and copies ran while one was open for 0% of the time, Pallas kernels for 0%

commit v1 on v0

v1 whole, which is shorter than its diff:
```python
import functools
import math

import jax
import jax.numpy as jnp
from jax import lax
from jax.experimental import pallas as pl
from jax.experimental.pallas import tpu as pltpu
from jax.sharding import PartitionSpec as P

TILE = 128
ITERS = 3
EPS_BLUR = 0.1
LOG2E = math.log2(math.e)
LOW = -1e30
MESH = pl.DeviceIdType.MESH
NT_DIMS = (((1,), (1,)), ((), ()))
NN_DIMS = (((1,), (0,)), ((), ()))


def mm(a, b, dims):
    return lax.dot_general(a, b, dims, preferred_element_type=jnp.float32)


def log2(x):
    return jnp.log(x) * LOG2E


def split2(x):
    hi = x.astype(jnp.bfloat16)
    lo = (x - hi.astype(jnp.float32)).astype(jnp.bfloat16)
    return hi, lo


def stack_hi_lo(row):
    hi = row.astype(jnp.bfloat16).astype(jnp.float32)
    lo = row - hi
    sub = lax.broadcasted_iota(jnp.int32, (8, TILE), 0)
    full_hi = jnp.broadcast_to(hi, (8, TILE))
    full_lo = jnp.broadcast_to(lo, (8, TILE))
    return jnp.where(sub == 0, full_hi, jnp.where(sub == 1, full_lo, 0.0)).astype(jnp.bfloat16)


def kernel(
    n_s, n_t, blocks, slots, feats,
    rows_s, cols_s, rid1, rid2, cid1, cid2, x_ref, y_ref, la_ref, lb_ref,
    a_out, b_out,
    xg, yg, lbg, xa, ya, ny, abc, tiles, slot_max, slot_sum, ridb, cidb,
    row_part, row_recv, a_full, a_cur, col_part, col_recv, b_cur, lb_full, part,
    sem_x, sem_y, sem_l, sem_ra, sem_rb, sem_c,
):
    s = lax.axis_index("src")
    t = lax.axis_index("tgt")
    rb = blocks // n_t
    cb = blocks // n_s
    kappa = 2.0 * LOG2E / (feats * EPS_BLUR)

    barrier = pltpu.get_barrier_semaphore()
    for d in range(1, n_t):
        pl.semaphore_signal(barrier, inc=1, device_id=(s, lax.rem(t + d, n_t)), device_id_type=MESH)
    for d in range(1, n_s):
        pl.semaphore_signal(barrier, inc=1, device_id=(lax.rem(s + d, n_s), t), device_id_type=MESH)
    pl.semaphore_wait(barrier, n_t + n_s - 2)

    def send(src, dst, sems, index, d, along_tgt):
        if along_tgt:
            dev = (s, lax.rem(t + d, n_t))
        else:
            dev = (lax.rem(s + d, n_s), t)
        copy = pltpu.make_async_remote_copy(
            src_ref=src, dst_ref=dst, send_sem=sems.at[(0, *index)], recv_sem=sems.at[(1, *index)],
            device_id=dev, device_id_type=MESH,
        )
        copy.start()
        return copy

    x_copies = {}
    y_copies = {}
    l_copies = {}
    for d in range(1, max(n_t, n_s)):
        if d < n_s:
            y_copies[d] = send(y_ref, yg.at[s], sem_y, (d,), d, False)
            l_copies[d] = send(lb_ref, lbg.at[s], sem_l, (d,), d, False)
        if d < n_t:
            x_copies[d] = send(x_ref, xg.at[t], sem_x, (d,), d, True)
    xg[t] = x_ref[...]
    yg[s] = y_ref[...]
    lbg[s] = lb_ref[...]

    ridb[...] = jnp.broadcast_to(rid2[...], ridb.shape)
    cidb[...] = jnp.broadcast_to(cid2[...], cidb.shape)

    ii = lax.broadcasted_iota(jnp.int32, (TILE, TILE), 0)
    jj = lax.broadcasted_iota(jnp.int32, (TILE, TILE), 1)
    in_low = jj < feats
    take = [
        jnp.where((ii == jj + h * feats) & in_low, 1.0, 0.0).astype(jnp.bfloat16) for h in range(2)
    ]
    half_ones = [
        jnp.where((ii // feats) == h, 1.0, 0.0).astype(jnp.bfloat16) for h in range(2)
    ]

    def unpack_x(owner):
        def body(q, carry):
            v = xg[owner, pl.ds(pl.multiple_of(q * TILE, TILE), TILE), :]
            for h in range(2):
                xa[owner * rb + h * (rb // 2) + q] = mm(v, take[h], NN_DIMS).astype(jnp.bfloat16)
            return carry
        lax.fori_loop(0, rb // 2, body, 0)

    def unpack_y(owner):
        def body(q, carry):
            v = yg[owner, pl.ds(pl.multiple_of(q * TILE, TILE), TILE), :]
            wide = v.astype(jnp.float32)
            hi, lo = split2(wide * wide)
            for h in range(2):
                b = owner * cb + h * (cb // 2) + q
                ya[b] = mm(v, take[h], NN_DIMS).astype(jnp.bfloat16)
                norm = mm(hi, half_ones[h], NN_DIMS) + mm(lo, half_ones[h], NN_DIMS)
                ny[b] = norm * (0.5 * kappa)
            return carry
        lax.fori_loop(0, cb // 2, body, 0)

    unpack_x(t)
    unpack_y(s)
    for d in range(1, max(n_t, n_s)):
        if d < n_s:
            y_copies[d].wait()
            l_copies[d].wait()
            unpack_y(lax.rem(s - d + n_s, n_s))
    for d in range(1, n_t):
        x_copies[d].wait()
        unpack_x(lax.rem(t - d + n_t, n_t))
    for o in range(n_s):
        lb_full[pl.ds(o * cb, cb), :] = lbg[o] * LOG2E

    unroll = 4
    zero = jnp.int32(0)

    def first_rows(g, carry):
        for q in range(unroll):
            k = g * unroll + q
            r = rows_s[k]
            c = cols_s[k]
            w = mm(ya[c], xa[r], NT_DIMS) * kappa - ny[c]
            m = jnp.max(w, axis=0, keepdims=True)
            slot_max[pl.ds(k, 1), :] = m
            slot_sum[pl.ds(k, 1), :] = jnp.sum(jnp.exp2(w - m), axis=0, keepdims=True)
        return carry

    def first_cols(g, carry):
        for q in range(unroll):
            k = g * unroll + q
            r = rows_s[k]
            c = cols_s[k]
            w = mm(xa[r], ya[c], NT_DIMS) * kappa + abc[r]
            m = jnp.max(w, axis=0, keepdims=True)
            e = jnp.exp2(w - m)
            slot_max[pl.ds(k, 1), :] = m
            slot_sum[pl.ds(k, 1), :] = jnp.sum(e, axis=0, keepdims=True)
            tiles[k] = e.astype(jnp.bfloat16)
        return carry

    def combine_lse(ids, out, per):
        def body(b, carry):
            high = jnp.where(ids[...] == b, slot_max[...], LOW)
            top = jnp.max(high, axis=0, keepdims=True)
            total = jnp.sum(slot_sum[...] * jnp.exp2(high - top), axis=0, keepdims=True)
            out[b // per, pl.ds(b % per, 1), :] = top + log2(total)
            return carry
        lax.fori_loop(0, blocks, body, 0)

    def combine_sum(ids1, out, n, per):
        which = lax.broadcasted_iota(jnp.int32, (blocks, slots), 0)
        onehot = jnp.where(which == ids1[...], 1.0, 0.0).astype(jnp.bfloat16)
        hi, lo = split2(slot_sum[...])
        full = mm(onehot, hi, NN_DIMS) + mm(onehot, lo, NN_DIMS)
        for o in range(n):
            out[o] = full[o * per:(o + 1) * per, :]

    def lse_of(values):
        top = functools.reduce(jnp.maximum, values)
        return top + log2(sum(jnp.exp2(v - top) for v in values))

    def rows_exchange(it, finish):
        copies = [
            send(row_part.at[it, lax.rem(t + d, n_t)], row_recv.at[it, d], sem_ra, (it, d), d, True)
            for d in range(1, n_t)
        ]
        for copy in copies:
            copy.wait()
        own = finish([row_part[it, t]] + [row_recv[it, d] for d in range(1, n_t)])
        a_full[it, t] = own
        copies = [
            send(a_full.at[it, t], a_full.at[it, t], sem_rb, (it, d), d, True) for d in range(1, n_t)
        ]
        for copy in copies:
            copy.wait()
        return own

    lax.fori_loop(0, slots // unroll, first_rows, 0)
    combine_lse(ridb, row_part.at[0], rb)
    la2 = la_ref[...] * LOG2E
    a_first = rows_exchange(0, lambda vs: la2 - lse_of(vs))
    for o in range(n_t):
        a_cur[pl.ds(o * rb, rb), :] = a_full[0, o]

    def spread(g, carry):
        for q in range(4):
            r = g * 4 + q
            abc[r] = jnp.transpose(jnp.broadcast_to(a_cur[pl.ds(r, 1), :], (TILE, TILE)))
        return carry
    lax.fori_loop(0, blocks // 4, spread, 0)

    lax.fori_loop(0, slots // unroll, first_cols, 0)
    combine_lse(cidb, col_part.at[0], cb)
    copies = [
        send(col_part.at[0], col_recv.at[0, d], sem_c, (0, d), d, False) for d in range(1, n_s)
    ]
    for copy in copies:
        copy.wait()
    for o in range(n_s):
        lse = lse_of([col_part[0, o]] + [col_recv[0, d, o] for d in range(1, n_s)])
        b_cur[pl.ds(o * cb, cb), :] = lb_full[pl.ds(o * cb, cb), :] - lse

    wide_unroll = 8

    def later_rows(g, carry):
        for q in range(wide_unroll):
            k = g * wide_unroll + q
            c = cols_s[k]
            w = jnp.exp2(jnp.minimum(slot_max[pl.ds(k, 1), :] + b_cur[pl.ds(c, 1), :], 100.0))
            got = mm(stack_hi_lo(w), tiles[k], NT_DIMS)
            slot_sum[pl.ds(k, 1), :] = got[0:1, :] + got[1:2, :]
        return carry

    def later_cols(g, carry):
        for q in range(wide_unroll):
            k = g * wide_unroll + q
            r = rows_s[k]
            c = cols_s[k]
            got = mm(stack_hi_lo(a_cur[pl.ds(r, 1), :]), tiles[k], NN_DIMS)
            f = jnp.exp2(jnp.minimum(slot_max[pl.ds(k, 1), :] + b_cur[pl.ds(c, 1), :], 60.0))
            slot_sum[pl.ds(k, 1), :] = (got[0:1, :] + got[1:2, :]) * f
        return carry

    for it in range(1, ITERS):
        lax.fori_loop(0, slots // wide_unroll, later_rows, 0)
        combine_sum(rid1, row_part.at[it], n_t, rb)
        own = rows_exchange(it, lambda vs: a_first + la2 - log2(sum(vs)))
        for o in range(n_t):
            a_cur[pl.ds(o * rb, rb), :] = jnp.exp2(a_full[it, o] - a_full[0, o])
        if it == ITERS - 1:
            a_out[...] = own
        lax.fori_loop(0, slots // wide_unroll, later_cols, 0)
        combine_sum(cid1, col_part.at[it], n_s, cb)
        if it < ITERS - 1:
            copies = [
                send(col_part.at[it], col_recv.at[it, d], sem_c, (it, d), d, False)
                for d in range(1, n_s)
            ]
            for copy in copies:
                copy.wait()
            for o in range(n_s):
                at = pl.ds(o * cb, cb)
                total = sum([col_part[it, o]] + [col_recv[it, d, o] for d in range(1, n_s)])
                b_cur[at, :] = b_cur[at, :] + lb_full[at, :] - log2(total)
        else:
            copies = [
                send(col_part.at[it, lax.rem(s + d, n_s)], part.at[d], sem_c, (it, d), d, False)
                for d in range(1, n_s)
            ]
            for copy in copies:
                copy.wait()
            total = sum([col_part[it, s]] + [part[d] for d in range(1, n_s)])
            at = pl.ds(pl.multiple_of(s * cb, cb), cb)
            b_out[...] = b_cur[at, :] + lb_full[at, :] - log2(total)


def halves(points):
    half = points.shape[0] // 2
    return jnp.concatenate([points[:half], points[half:]], axis=1)


def local(n_s, n_t, sources, targets, log_src, log_tgt, tile_rows, tile_cols, tile_count):
    feats = sources.shape[1]
    slots = tile_rows.shape[-1]
    blocks = sources.shape[0] * n_t // TILE
    rb, cb = blocks // n_t, blocks // n_s
    rows = tile_rows.reshape(-1)
    cols = tile_cols.reshape(-1)
    live = lax.iota(jnp.int32, slots) < tile_count.reshape(())
    rid = jnp.where(live, rows, -1)
    cid = jnp.where(live, cols, -1)
    vm = pl.BlockSpec(memory_space=pltpu.VMEM)
    sm = pl.BlockSpec(memory_space=pltpu.SMEM)
    f32, bf16, i32 = jnp.float32, jnp.bfloat16, jnp.int32
    dma = pltpu.SemaphoreType.DMA
    xp, yp = halves(sources), halves(targets)
    a_own, b_own = pl.pallas_call(
        functools.partial(kernel, n_s, n_t, blocks, slots, feats),
        out_shape=(
            jax.ShapeDtypeStruct((rb, TILE), f32),
            jax.ShapeDtypeStruct((cb, TILE), f32),
        ),
        in_specs=[sm, sm] + [vm] * 8,
        out_specs=(vm, vm),
        scratch_shapes=[
            pltpu.VMEM((n_t, *xp.shape), bf16),
            pltpu.VMEM((n_s, *yp.shape), bf16),
            pltpu.VMEM((n_s, cb, TILE), f32),
            pltpu.VMEM((blocks, TILE, TILE), bf16),
            pltpu.VMEM((blocks, TILE, TILE), bf16),
            pltpu.VMEM((blocks, TILE, TILE), f32),
            pltpu.VMEM((blocks, TILE, TILE), f32),
            pltpu.VMEM((slots, TILE, TILE), bf16),
            pltpu.VMEM((slots, TILE), f32),
            pltpu.VMEM((slots, TILE), f32),
            pltpu.VMEM((slots, TILE), i32),
            pltpu.VMEM((slots, TILE), i32),
            pltpu.VMEM((ITERS, n_t, rb, TILE), f32),
            pltpu.VMEM((ITERS, n_t, rb, TILE), f32),
            pltpu.VMEM((ITERS, n_t, rb, TILE), f32),
            pltpu.VMEM((blocks, TILE), f32),
            pltpu.VMEM((ITERS, n_s, cb, TILE), f32),
            pltpu.VMEM((ITERS - 1, n_s, n_s, cb, TILE), f32),
            pltpu.VMEM((blocks, TILE), f32),
            pltpu.VMEM((blocks, TILE), f32),
            pltpu.VMEM((n_s, cb, TILE), f32),
            dma((2, n_t)),
            dma((2, n_s)),
            dma((2, n_s)),
            dma((2, ITERS, n_t)),
            dma((2, ITERS, n_t)),
            dma((2, ITERS, n_s)),
        ],
        compiler_params=pltpu.CompilerParams(
            collective_id=0, has_side_effects=True, vmem_limit_bytes=48 * 2**20
        ),
        cost_estimate=pl.CostEstimate(
            flops=12 * slots * TILE**3, bytes_accessed=2**20, transcendentals=2 * slots * TILE**2
        ),
    )(
        rows, cols, rid.reshape(1, -1), rid.reshape(-1, 1), cid.reshape(1, -1), cid.reshape(-1, 1),
        xp, yp, log_src.reshape(rb, TILE), log_tgt.reshape(cb, TILE),
    )
    scale = EPS_BLUR / LOG2E
    return tuple(
        own.reshape(-1) * scale + jnp.sum(points.astype(f32) ** 2, axis=-1) * (1.0 / feats)
        for own, points in ((a_own, sources), (b_own, targets))
    )


def solution(mesh):
    in_specs = (
        P(("src", "tgt"), None),
        P(("src", "tgt"), None),
        P(("src", "tgt")),
        P(("src", "tgt")),
        P("src", "tgt", None),
        P("src", "tgt", None),
        P("src", "tgt"),
    )
    out_specs = (P(("src", "tgt")), P(("src", "tgt")))
    body = functools.partial(local, mesh.shape["src"], mesh.shape["tgt"])
    return jax.shard_map(body, mesh=mesh, in_specs=in_specs, out_specs=out_specs, check_vma=False)
```

time: 1330 us -> 147 us (0.11)
  local copies, waits for them, and re-layouts: 647 us -> 4.63 us
  blocking collectives: 271 us -> 0 us
  matrix products: 181 us -> 0 us
  other arithmetic: 177 us -> 1.61 us
  Pallas kernels: 0 us -> 139 us
  waiting for transfers between devices: 28.7 us -> 0 us
  between operations: 15 us -> 1.42 us
    gather x576 -> x0, local copies, waits for them, and re-layouts: 640 us -> none  [the longest x96 213 us: visit(): far_blocks[far_index]]
    dot_general x96 -> x0, matrix products: 181 us -> none  [tile_scores(): jnp.einsum('kif,kjf->kij', near_points, far_points, preferred_element_typ...]
    pallas_call x0 -> x1, Pallas kernels: none -> 139 us  [local(): pl.pallas_call(functools.partial(kernel, n_s, n_t, blocks, slots, feats),...]
    pmax x6 -> x0, blocking collectives: 129 us -> none  [the longest x3 79.7 us: settle(): peak_all = lax.pmax(highest, 'tgt')]
    psum x6 -> x0, blocking collectives: 120 us -> none  [the longest x3 77.8 us: settle(): sum_all = lax.psum(summed * jnp.exp(highest - peak_all), 'tgt')]
    another operation x96 -> x0, other arithmetic: 67.9 us -> none  [fold_stats(): new_high = highest.at[near_index].max(tile_high)]
    scatter-add x96 -> x0, other arithmetic: 67.9 us -> none  [fold_stats(): added = jnp.zeros_like(summed).at[near_index].add(jnp.sum(weights, axis=2))]
    all_gather x2 -> x0, waiting for transfers between devices: 27.3 us -> none  [the longest x1 21.3 us: local(): lax.all_gather(sources, 'tgt', axis=0, tiled=True)]
  transfers between devices with their start and end apart: 2 -> 0, of which waited for: 2 -> 0; matrix products, arithmetic and copies ran while one was open for 0% -> 0% of each run, Pallas kernels for 0% -> 0%
where the time goes in v1:
time: 147 us
  Pallas kernels  139 us (95%)
  local copies, waits for them, and re-layouts  4.63 us (3%)
  other arithmetic  1.61 us (1%)
    pallas_call x1, Pallas kernels, local(): pl.pallas_call(functools.partial(kernel, n_s, n_t, blocks, slots, feats),...  139 us
    unnamed x16, local copies, waits for them, and re-layouts  3.37 us

profile of v1, /device:TPU:0, one launch (start us, length us, event | category | flops | bytes accessed | tf_op | source)
XLA Modules:
  0.0 147.1 jit_solution(9478907539169844153)
XLA Ops:
  0.6 1.0 fusion.2
  1.6 0.2 copy.21
  1.8 0.2 copy.22
  2.0 0.0 copy-start.5
  2.0 0.1 pad_maximum_fusion.y_ref
  2.1 0.7 copy-done.5
  2.9 0.1 copy.19
  3.0 0.1 copy.20
  3.1 0.1 pad_maximum_fusion.1.x_ref
  3.9 0.0 copy-start
  3.9 0.7 copy-done
  4.6 0.1 copy.13
  4.7 0.0 copy-start.1
  4.8 0.7 copy-done.1
  5.4 0.1 copy.14
  5.6 0.0 copy-start.2
  5.6 0.0 copy-start.3
  5.6 0.7 copy-done.2
  6.3 0.0 copy-done.3
  6.3 0.0 copy-start.4
  6.3 139.4 %shard_map.86 = (f32[8,128]{1,0:T(8,128)S(1)}, f32[16,128]{1,0:T(8,128)S(1)}) custom-call(s32[256]{0:T(256)S(1)} %bitcast.18, s32[256]{0:T(256)S(1)} %bitcast.20, s32[1,256]{1,0:T(1,128)S(1)} %get-tuple-element.13.rid1, s32[256,1]{1,0:T(8,128)S(1)} %get-tuple-element.11.rid2, s32[1,256]{1,0:T(1,128)S(1)} %get-tuple-element.12.cid1, ...), custom_call_target="tpu_custom_call" | custom-call | flops 6442450944 | bytes 1048576 | tf_op jit(solution)/shard_map/pallas_call | solution.py:300
  145.8 0.0 copy-done.4
  145.8 0.1 multiply_reduce_fusion
  145.9 0.6 bitcast_add_fusion
  146.5 0.6 bitcast_add_fusion.1
  (4 shorter events, 0.1 us)
Async XLA Ops:
  2.0 0.9 copy-start.5
  3.9 0.7 copy-start
  4.7 0.7 copy-start.1
  5.6 0.7 copy-start.2
  5.6 0.7 copy-start.3
  6.3 139.5 %copy-start.4 = (bf16[2048,64]{0,1:T(8,128)(2,1)S(1)}, bf16[2048,64]{0,1:T(8,128)(2,1)}, u32[]{:S(2)}) copy-start(bf16[2048,64]{0,1:T(8,128)(2,1)} %param.8) | copy-start | bytes 786436

commit v2 on v1

--- a/solution.py
+++ b/solution.py
@@ -43,11 +43,12 @@
 
 def kernel(
     n_s, n_t, blocks, slots, feats,
-    rows_s, cols_s, rid1, rid2, cid1, cid2, x_ref, y_ref, la_ref, lb_ref,
+    rows_s, cols_s, count_s, rows_v, cols_v, x_ref, y_ref, la_ref, lb_ref,
     a_out, b_out,
-    xg, yg, lbg, xa, ya, ny, abc, tiles, slot_max, slot_sum, ridb, cidb,
-    row_part, row_recv, a_full, a_cur, col_part, col_recv, b_cur, lb_full, part,
-    sem_x, sem_y, sem_l, sem_ra, sem_rb, sem_c,
+    xg, yg, lag, lbg, xa, ya, ny, abc, tiles, slot_max, slot_sum, ridb, cidb, tops,
+    row_part, row_recv, a_full, a_cur, col_part, col_recv, b_cur, mass, lb_full,
+    row_sums, row_sums_in, col_sums, col_sums_in, last_part, last_in,
+    sem_x, sem_f, sem_y, sem_la, sem_l, sem_ra, sem_rb, sem_r, sem_c,
 ):
     s = lax.axis_index("src")
     t = lax.axis_index("tgt")
@@ -74,21 +75,41 @@
         copy.start()
         return copy
 
-    x_copies = {}
-    y_copies = {}
-    l_copies = {}
-    for d in range(1, max(n_t, n_s)):
-        if d < n_s:
-            y_copies[d] = send(y_ref, yg.at[s], sem_y, (d,), d, False)
-            l_copies[d] = send(lb_ref, lbg.at[s], sem_l, (d,), d, False)
-        if d < n_t:
-            x_copies[d] = send(x_ref, xg.at[t], sem_x, (d,), d, True)
+    n_z = n_t // 2
+    mate = t + 1 - 2 * lax.rem(t, 2)
+    to_mate = 0
+
+    def before(owner, dz):
+        return lax.rem(owner - 2 * dz + n_t, n_t)
+
+    def send_x(owner, sems, index, dest):
+        copy = pltpu.make_async_remote_copy(
+            src_ref=x_ref if owner is None else xg.at[owner],
+            dst_ref=xg.at[t if owner is None else owner],
+            send_sem=sems.at[0, index], recv_sem=sems.at[1, index],
+            device_id=(s, dest), device_id_type=MESH,
+        )
+        copy.start()
+        return copy
+
+    x_copies = {dz: send_x(None, sem_x, dz, lax.rem(t + 2 * dz, n_t)) for dz in range(1, n_z)}
+    y_copies = {d: send(y_ref, yg.at[s], sem_y, (d,), d, False) for d in range(1, n_s)}
+    x_copies[to_mate] = send_x(None, sem_x, to_mate, mate)
+    small = [send(lb_ref, lbg.at[s], sem_l, (d,), d, False) for d in range(1, n_s)]
+    small += [send(la_ref, lag.at[t], sem_la, (d,), d, True) for d in range(1, n_t)]
     xg[t] = x_ref[...]
     yg[s] = y_ref[...]
+    lag[t] = la_ref[...]
     lbg[s] = lb_ref[...]
 
-    ridb[...] = jnp.broadcast_to(rid2[...], ridb.shape)
-    cidb[...] = jnp.broadcast_to(cid2[...], cidb.shape)
+    slot_at = lax.broadcasted_iota(jnp.int32, (1, slots), 1)
+    rid1 = jnp.where(slot_at < count_s[0, 0], rows_v[...], -1)
+    cid1 = jnp.where(slot_at < count_s[0, 0], cols_v[...], -1)
+    for ids, wide in ((rid1, ridb), (cid1, cidb)):
+        for h in range(slots // TILE):
+            at = slice(h * TILE, (h + 1) * TILE)
+            flat = jnp.broadcast_to(ids[:, at].astype(jnp.float32), (TILE, TILE))
+            wide[at, :] = jnp.transpose(flat)
 
     ii = lax.broadcasted_iota(jnp.int32, (TILE, TILE), 0)
     jj = lax.broadcasted_iota(jnp.int32, (TILE, TILE), 1)
@@ -123,19 +144,31 @@
 
     unpack_x(t)
     unpack_y(s)
-    for d in range(1, max(n_t, n_s)):
+    x_copies[to_mate].wait()
+    unpack_x(mate)
+    forwards = {}
+    for d in range(1, max(n_z, n_s)):
+        if d < n_z:
+            x_copies[d].wait_recv()
+            forwards[d] = send_x(before(t, d), sem_f, d, mate)
+            unpack_x(before(t, d))
         if d < n_s:
             y_copies[d].wait()
-            l_copies[d].wait()
             unpack_y(lax.rem(s - d + n_s, n_s))
-    for d in range(1, n_t):
-        x_copies[d].wait()
-        unpack_x(lax.rem(t - d + n_t, n_t))
+    for d in range(1, n_z):
+        forwards[d].wait_recv()
+        unpack_x(before(mate, d))
+    for d in range(1, n_z):
+        x_copies[d].wait_send()
+        forwards[d].wait_send()
+    for copy in small:
+        copy.wait()
+    for o in range(n_t):
+        mass[pl.ds(o * rb, rb), :] = jnp.exp(lag[o])
     for o in range(n_s):
         lb_full[pl.ds(o * cb, cb), :] = lbg[o] * LOG2E
 
-    unroll = 4
-    zero = jnp.int32(0)
+    unroll = 16
 
     def first_rows(g, carry):
         for q in range(unroll):
@@ -161,49 +194,60 @@
             tiles[k] = e.astype(jnp.bfloat16)
         return carry
 
-    def combine_lse(ids, out, per):
-        def body(b, carry):
-            high = jnp.where(ids[...] == b, slot_max[...], LOW)
-            top = jnp.max(high, axis=0, keepdims=True)
-            total = jnp.sum(slot_sum[...] * jnp.exp2(high - top), axis=0, keepdims=True)
-            out[b // per, pl.ds(b % per, 1), :] = top + log2(total)
+    group = 8
+
+    def by_block(ids1, values):
+        which = lax.broadcasted_iota(jnp.int32, (blocks, slots), 0)
+        onehot = jnp.where(which == ids1, 1.0, 0.0).astype(jnp.bfloat16)
+        hi, lo = split2(values)
+        return mm(onehot, hi, NN_DIMS) + mm(onehot, lo, NN_DIMS)
+
+    def combine_lse(ids, ids1):
+        def body(g, carry):
+            base = (g * group).astype(jnp.float32)
+            tall = [jnp.full((8, TILE), LOW, jnp.float32)] * group
+            for ch in range(slots // 8):
+                at = slice(ch * 8, ch * 8 + 8)
+                offset = ids[at, :] - base
+                high = slot_max[at, :]
+                for b in range(group):
+                    tall[b] = jnp.maximum(tall[b], jnp.where(offset == b, high, LOW))
+            for b in range(group):
+                tops[pl.ds(g * group + b, 1), :] = jnp.max(tall[b], axis=0, keepdims=True)
             return carry
-        lax.fori_loop(0, blocks, body, 0)
-
-    def combine_sum(ids1, out, n, per):
-        which = lax.broadcasted_iota(jnp.int32, (blocks, slots), 0)
-        onehot = jnp.where(which == ids1[...], 1.0, 0.0).astype(jnp.bfloat16)
-        hi, lo = split2(slot_sum[...])
-        full = mm(onehot, hi, NN_DIMS) + mm(onehot, lo, NN_DIMS)
-        for o in range(n):
-            out[o] = full[o * per:(o + 1) * per, :]
+        lax.fori_loop(0, blocks // group, body, 0)
+        top = tops[...]
+        lane = lax.broadcasted_iota(jnp.int32, (slots, TILE), 1).astype(jnp.float32)
+        pick = jnp.where(ids[...] == lane, 1.0, 0.0)[:, :blocks].astype(jnp.bfloat16)
+        hi, rest = split2(top)
+        rest = top - hi.astype(jnp.float32)
+        mid, low = split2(rest)
+        seen = mm(pick, hi, NN_DIMS) + mm(pick, mid, NN_DIMS) + mm(pick, low, NN_DIMS)
+        scaled = slot_sum[...] * jnp.exp2(jnp.minimum(slot_max[...] - seen, 1.0))
+        return top + log2(by_block(ids1, scaled))
 
     def lse_of(values):
         top = functools.reduce(jnp.maximum, values)
         return top + log2(sum(jnp.exp2(v - top) for v in values))
 
-    def rows_exchange(it, finish):
-        copies = [
-            send(row_part.at[it, lax.rem(t + d, n_t)], row_recv.at[it, d], sem_ra, (it, d), d, True)
-            for d in range(1, n_t)
-        ]
-        for copy in copies:
-            copy.wait()
-        own = finish([row_part[it, t]] + [row_recv[it, d] for d in range(1, n_t)])
-        a_full[it, t] = own
-        copies = [
-            send(a_full.at[it, t], a_full.at[it, t], sem_rb, (it, d), d, True) for d in range(1, n_t)
-        ]
-        for copy in copies:
-            copy.wait()
-        return own
-
     lax.fori_loop(0, slots // unroll, first_rows, 0)
-    combine_lse(ridb, row_part.at[0], rb)
+    lse = combine_lse(ridb, rid1)
+    for o in range(n_t):
+        row_part[o] = lse[o * rb:(o + 1) * rb, :]
+    copies = [
+        send(row_part.at[lax.rem(t + d, n_t)], row_recv.at[d], sem_ra, (d,), d, True)
+        for d in range(1, n_t)
+    ]
+    for copy in copies:
+        copy.wait()
     la2 = la_ref[...] * LOG2E
-    a_first = rows_exchange(0, lambda vs: la2 - lse_of(vs))
+    a_first = la2 - lse_of([row_part[t]] + [row_recv[d] for d in range(1, n_t)])
+    a_full[t] = a_first
+    copies = [send(a_full.at[t], a_full.at[t], sem_rb, (d,), d, True) for d in range(1, n_t)]
+    for copy in copies:
+        copy.wait()
     for o in range(n_t):
-        a_cur[pl.ds(o * rb, rb), :] = a_full[0, o]
+        a_cur[pl.ds(o * rb, rb), :] = a_full[o]
 
     def spread(g, carry):
         for q in range(4):
@@ -213,17 +257,14 @@
     lax.fori_loop(0, blocks // 4, spread, 0)
 
     lax.fori_loop(0, slots // unroll, first_cols, 0)
-    combine_lse(cidb, col_part.at[0], cb)
-    copies = [
-        send(col_part.at[0], col_recv.at[0, d], sem_c, (0, d), d, False) for d in range(1, n_s)
-    ]
+    col_part[...] = combine_lse(cidb, cid1)
+    copies = [send(col_part, col_recv.at[d], sem_c, (0, d), d, False) for d in range(1, n_s)]
     for copy in copies:
         copy.wait()
-    for o in range(n_s):
-        lse = lse_of([col_part[0, o]] + [col_recv[0, d, o] for d in range(1, n_s)])
-        b_cur[pl.ds(o * cb, cb), :] = lb_full[pl.ds(o * cb, cb), :] - lse
-
-    wide_unroll = 8
+    lse = lse_of([col_part[...]] + [col_recv[d] for d in range(1, n_s)])
+    b_cur[...] = lb_full[...] - lse
+
+    wide_unroll = 16
 
     def later_rows(g, carry):
         for q in range(wide_unroll):
@@ -244,36 +285,38 @@
             slot_sum[pl.ds(k, 1), :] = (got[0:1, :] + got[1:2, :]) * f
         return carry
 
+    def totals(own, sums, sums_in, sems, it, n, along_tgt):
+        sums[it - 1] = own.astype(jnp.bfloat16)
+        copies = [
+            send(sums.at[it - 1], sums_in.at[it - 1, d], sems, (it, d), d, along_tgt)
+            for d in range(1, n)
+        ]
+        for copy in copies:
+            copy.wait()
+        return own + sum(sums_in[it - 1, d].astype(jnp.float32) for d in range(1, n))
+
     for it in range(1, ITERS):
         lax.fori_loop(0, slots // wide_unroll, later_rows, 0)
-        combine_sum(rid1, row_part.at[it], n_t, rb)
-        own = rows_exchange(it, lambda vs: a_first + la2 - log2(sum(vs)))
-        for o in range(n_t):
-            a_cur[pl.ds(o * rb, rb), :] = jnp.exp2(a_full[it, o] - a_full[0, o])
+        own = by_block(rid1, slot_sum[...])
+        a_cur[...] = mass[...] / totals(own, row_sums, row_sums_in, sem_r, it, n_t, True)
         if it == ITERS - 1:
-            a_out[...] = own
+            a_out[...] = a_first + log2(a_cur[pl.ds(t * rb, rb), :])
         lax.fori_loop(0, slots // wide_unroll, later_cols, 0)
-        combine_sum(cid1, col_part.at[it], n_s, cb)
+        own = by_block(cid1, slot_sum[...])
         if it < ITERS - 1:
+            total = totals(own, col_sums, col_sums_in, sem_c, it, n_s, False)
+            b_cur[...] = b_cur[...] + lb_full[...] - log2(total)
+        else:
+            for o in range(n_s):
+                last_part[o] = own[o * cb:(o + 1) * cb, :]
             copies = [
-                send(col_part.at[it], col_recv.at[it, d], sem_c, (it, d), d, False)
+                send(last_part.at[lax.rem(s + d, n_s)], last_in.at[d], sem_c, (it, d), d, False)
                 for d in range(1, n_s)
             ]
             for copy in copies:
                 copy.wait()
-            for o in range(n_s):
-                at = pl.ds(o * cb, cb)
-                total = sum([col_part[it, o]] + [col_recv[it, d, o] for d in range(1, n_s)])
-                b_cur[at, :] = b_cur[at, :] + lb_full[at, :] - log2(total)
-        else:
-            copies = [
-                send(col_part.at[it, lax.rem(s + d, n_s)], part.at[d], sem_c, (it, d), d, False)
-                for d in range(1, n_s)
-            ]
-            for copy in copies:
-                copy.wait()
-            total = sum([col_part[it, s]] + [part[d] for d in range(1, n_s)])
-            at = pl.ds(pl.multiple_of(s * cb, cb), cb)
+            total = last_part[s] + sum(last_in[d] for d in range(1, n_s))
+            at = pl.ds(s * cb, cb)
             b_out[...] = b_cur[at, :] + lb_full[at, :] - log2(total)
 
 
@@ -289,9 +332,6 @@
     rb, cb = blocks // n_t, blocks // n_s
     rows = tile_rows.reshape(-1)
     cols = tile_cols.reshape(-1)
-    live = lax.iota(jnp.int32, slots) < tile_count.reshape(())
-    rid = jnp.where(live, rows, -1)
-    cid = jnp.where(live, cols, -1)
     vm = pl.BlockSpec(memory_space=pltpu.VMEM)
     sm = pl.BlockSpec(memory_space=pltpu.SMEM)
     f32, bf16, i32 = jnp.float32, jnp.bfloat16, jnp.int32
@@ -303,11 +343,12 @@
             jax.ShapeDtypeStruct((rb, TILE), f32),
             jax.ShapeDtypeStruct((cb, TILE), f32),
         ),
-        in_specs=[sm, sm] + [vm] * 8,
+        in_specs=[sm] * 3 + [vm] * 6,
         out_specs=(vm, vm),
         scratch_shapes=[
             pltpu.VMEM((n_t, *xp.shape), bf16),
             pltpu.VMEM((n_s, *yp.shape), bf16),
+            pltpu.VMEM((n_t, rb, TILE), f32),
             pltpu.VMEM((n_s, cb, TILE), f32),
             pltpu.VMEM((blocks, TILE, TILE), bf16),
             pltpu.VMEM((blocks, TILE, TILE), bf16),
@@ -316,21 +357,31 @@
             pltpu.VMEM((slots, TILE, TILE), bf16),
             pltpu.VMEM((slots, TILE), f32),
             pltpu.VMEM((slots, TILE), f32),
-            pltpu.VMEM((slots, TILE), i32),
-            pltpu.VMEM((slots, TILE), i32),
-            pltpu.VMEM((ITERS, n_t, rb, TILE), f32),
-            pltpu.VMEM((ITERS, n_t, rb, TILE), f32),
-            pltpu.VMEM((ITERS, n_t, rb, TILE), f32),
-            pltpu.VMEM((blocks, TILE), f32),
-            pltpu.VMEM((ITERS, n_s, cb, TILE), f32),
-            pltpu.VMEM((ITERS - 1, n_s, n_s, cb, TILE), f32),
-            pltpu.VMEM((blocks, TILE), f32),
-            pltpu.VMEM((blocks, TILE), f32),
+            pltpu.VMEM((slots, TILE), f32),
+            pltpu.VMEM((slots, TILE), f32),
+            pltpu.VMEM((blocks, TILE), f32),
+            pltpu.VMEM((n_t, rb, TILE), f32),
+            pltpu.VMEM((n_t, rb, TILE), f32),
+            pltpu.VMEM((n_t, rb, TILE), f32),
+            pltpu.VMEM((blocks, TILE), f32),
+            pltpu.VMEM((blocks, TILE), f32),
+            pltpu.VMEM((n_s, blocks, TILE), f32),
+            pltpu.VMEM((blocks, TILE), f32),
+            pltpu.VMEM((blocks, TILE), f32),
+            pltpu.VMEM((blocks, TILE), f32),
+            pltpu.VMEM((ITERS - 1, blocks, TILE), bf16),
+            pltpu.VMEM((ITERS - 1, n_t, blocks, TILE), bf16),
+            pltpu.VMEM((ITERS - 1, blocks, TILE), bf16),
+            pltpu.VMEM((ITERS - 1, n_s, blocks, TILE), bf16),
+            pltpu.VMEM((n_s, cb, TILE), f32),
             pltpu.VMEM((n_s, cb, TILE), f32),
             dma((2, n_t)),
+            dma((2, n_t)),
             dma((2, n_s)),
+            dma((2, n_t)),
             dma((2, n_s)),
-            dma((2, ITERS, n_t)),
+            dma((2, n_t)),
+            dma((2, n_t)),
             dma((2, ITERS, n_t)),
             dma((2, ITERS, n_s)),
         ],
@@ -341,7 +392,7 @@
             flops=12 * slots * TILE**3, bytes_accessed=2**20, transcendentals=2 * slots * TILE**2
         ),
     )(
-        rows, cols, rid.reshape(1, -1), rid.reshape(-1, 1), cid.reshape(1, -1), cid.reshape(-1, 1),
+        rows, cols, tile_count, rows.reshape(1, -1), cols.reshape(1, -1),
         xp, yp, log_src.reshape(rb, TILE), log_tgt.reshape(cb, TILE),
     )
     scale = EPS_BLUR / LOG2E

time: 147 us -> 103 us (0.70)
  Pallas kernels: 139 us -> 96.3 us
  local copies, waits for them, and re-layouts: 4.63 us -> 3 us
    pallas_call x1, Pallas kernels: 139 us -> 96.3 us  [local(): pl.pallas_call(functools.partial(kernel, n_s, n_t, blocks, slots, feats),...]
where the time goes in v2:
time: 103 us; the launch traced here: 102 us
  Pallas kernels  96.3 us (93%)
  local copies, waits for them, and re-layouts  3 us (3%)
  other arithmetic  1.57 us (2%)
  between operations  1.41 us (1%)
    pallas_call x1, Pallas kernels, local(): pl.pallas_call(functools.partial(kernel, n_s, n_t, blocks, slots, feats),...  96.3 us

profile of v2, /device:TPU:0, one launch (start us, length us, event | category | flops | bytes accessed | tf_op | source)
XLA Modules:
  0.0 102.3 jit_solution(491995865646005463)
XLA Ops:
  0.6 1.0 fusion
  1.6 0.2 copy.15
  1.8 0.2 copy.16
  2.0 0.0 copy-start.5
  2.0 0.1 pad_maximum_fusion.y_ref
  2.1 0.7 copy-done.5
  2.9 0.1 copy.13
  3.0 0.1 copy.14
  3.1 0.0 copy-start.3
  3.2 0.1 pad_maximum_fusion.1.x_ref
  3.3 0.0 copy-start
  3.9 0.0 copy-start.1
  4.0 0.0 copy-start.2
  4.0 0.0 copy-done.3
  4.0 0.0 copy-done
  4.0 0.6 copy-done.1
  4.6 0.0 copy-done.2
  4.6 0.0 copy-start.4
  4.6 96.3 %shard_map.86 = (f32[8,128]{1,0:T(8,128)S(1)}, f32[16,128]{1,0:T(8,128)S(1)}) custom-call(s32[256]{0:T(256)S(1)} %bitcast.12, s32[256]{0:T(256)S(1)} %bitcast.14, s32[1,1]{1,0:T(1,128)S(6)} %copy.17.count_s, s32[1,256]{1,0:T(1,128)S(1)} %bitcast.13, s32[1,256]{1,0:T(1,128)S(1)} %bitcast.15, bf16[512,128]{1,0:T(8,128)(2,1)S(1)} %pad_maximum_fusion.1.x_ref, ...), custom_call_target="tpu_custom_call" | custom-call | flops 6442450944 | bytes 1048576 | tf_op jit(solution)/shard_map/pallas_call | solution.py:340
  100.9 0.0 copy-done.4
  101.0 0.1 multiply_reduce_fusion
  101.0 0.6 bitcast_add_fusion
  101.7 0.6 bitcast_add_fusion.1
  (2 shorter events, 0.0 us)
Async XLA Ops:
  2.0 0.9 copy-start.5
  3.1 0.8 copy-start.3
  3.3 0.7 copy-start
  3.9 0.7 copy-start.1
  4.0 0.7 copy-start.2
  4.6 96.3 %copy-start.4 = (bf16[2048,64]{0,1:T(8,128)(2,1)S(1)}, bf16[2048,64]{0,1:T(8,128)(2,1)}, u32[]{:S(2)}) copy-start(bf16[2048,64]{0,1:T(8,128)(2,1)} %param.8) | copy-start | bytes 786436

commit v3 on v2

--- a/solution.py
+++ b/solution.py
@@ -168,7 +168,7 @@
     for o in range(n_s):
         lb_full[pl.ds(o * cb, cb), :] = lbg[o] * LOG2E
 
-    unroll = 16
+    unroll = 32
 
     def first_rows(g, carry):
         for q in range(unroll):
@@ -264,7 +264,7 @@
     lse = lse_of([col_part[...]] + [col_recv[d] for d in range(1, n_s)])
     b_cur[...] = lb_full[...] - lse
 
-    wide_unroll = 16
+    wide_unroll = 32
 
     def later_rows(g, carry):
         for q in range(wide_unroll):

time: 103 us -> 95.9 us (0.931)
  Pallas kernels: 96.3 us -> 89.7 us
    pallas_call x1, Pallas kernels: 96.3 us -> 89.7 us  [local(): pl.pallas_call(functools.partial(kernel, n_s, n_t, blocks, slots, feats),...]
where the time goes in v3:
time: 95.9 us; the launch traced here: 95.7 us
  Pallas kernels  89.7 us (94%)
  local copies, waits for them, and re-layouts  3 us (3%)
  other arithmetic  1.57 us (2%)
  between operations  1.41 us (1%)
    pallas_call x1, Pallas kernels, local(): pl.pallas_call(functools.partial(kernel, n_s, n_t, blocks, slots, feats),...  89.7 us
    unnamed x16, local copies, waits for them, and re-layouts  2.01 us

profile of v3, /device:TPU:0, one launch (start us, length us, event | category | flops | bytes accessed | tf_op | source)
XLA Modules:
  0.0 95.7 jit_solution(3522361149033797206)
XLA Ops:
  0.6 1.0 %fusion = (bf16[1024,64]{0,1:T(8,128)(2,1)S(1)}, bf16[1024,64]{0,1:T(8,128)(2,1)S(1)}) fusion(bf16[2048,64]{0,1:T(8,128)(2,1)} %param.8), kind=kLoop, calls=%fused_computation.6 | loop fusion | bytes 524288 | tf_op jit(solution)/shard_map/slice | solution.py:325
  1.6 0.2 copy.15
  1.8 0.2 copy.16
  2.0 0.0 copy-start.5
  2.0 0.1 pad_maximum_fusion.y_ref
  2.1 0.7 copy-done.5
  2.9 0.1 copy.13
  3.0 0.1 copy.14
  3.1 0.0 copy-start.3
  3.2 0.1 pad_maximum_fusion.1.x_ref
  3.3 0.0 copy-start
  3.9 0.0 copy-start.1
  4.0 0.0 copy-start.2
  4.0 0.0 copy-done.3
  4.0 0.0 copy-done
  4.0 0.6 copy-done.1
  4.6 0.0 copy-done.2
  4.6 0.0 copy-start.4
  4.6 89.7 %shard_map.86 = (f32[8,128]{1,0:T(8,128)S(1)}, f32[16,128]{1,0:T(8,128)S(1)}) custom-call(s32[256]{0:T(256)S(1)} %bitcast.12, s32[256]{0:T(256)S(1)} %bitcast.14, s32[1,1]{1,0:T(1,128)S(6)} %copy.17.count_s, s32[1,256]{1,0:T(1,128)S(1)} %bitcast.13, s32[1,256]{1,0:T(1,128)S(1)} %bitcast.15, bf16[512,128]{1,0:T(8,128)(2,1)S(1)} %pad_maximum_fusion.1.x_ref, ...), custom_call_target="tpu_custom_call" | custom-call | flops 6442450944 | bytes 1048576 | tf_op jit(solution)/shard_map/pallas_call | solution.py:340
  94.4 0.0 copy-done.4
  94.4 0.1 multiply_reduce_fusion
  94.5 0.6 bitcast_add_fusion
  95.1 0.6 bitcast_add_fusion.1
  (2 shorter events, 0.0 us)
Async XLA Ops:
  2.0 0.9 copy-start.5
  3.1 0.8 copy-start.3
  3.3 0.7 copy-start
  3.9 0.7 copy-start.1
  4.0 0.7 copy-start.2
  4.6 89.7 %copy-start.4 = (bf16[2048,64]{0,1:T(8,128)(2,1)S(1)}, bf16[2048,64]{0,1:T(8,128)(2,1)}, u32[]{:S(2)}) copy-start(bf16[2048,64]{0,1:T(8,128)(2,1)} %param.8) | copy-start | bytes 786436
